TPU v7x, 256 devices: a whole 4x4x8 slice. The times are simulated.
256 devices in a mesh: band: 8 (over z_hi, core), row: 32 (over y, z_lo, x).
Axes of the slice: x: 4, y: 4, z: 8 (z_hi: 4, z_lo: 2; z = z_hi * 2 + z_lo), core: 2. Of those that a mesh axis runs over, the one named last changes fastest.
Arguments:
- observed: float32 [128, 512, 512], P('band', 'row'), may hold values from -6 to 6
- image: float32 [128, 512, 512], P('band', 'row'), may hold values from -6 to 6
- vector_field: float32 [2, 128, 512, 512], P(None, 'band', 'row'), may hold values from -6 to 6
- dual_grad: float32 [2, 128, 512, 512], P(None, 'band', 'row'), may hold values from -18 to 18
- dual_sym: float32 [3, 128, 512, 512], P(None, 'band', 'row'), may hold values from -18 to 18
- dual_data: float32 [128, 512, 512], P('band', 'row'), may hold values from -6 to 6
- kernels: float32 [16, 15, 15], replicated, may hold values from 0 to 0.03
- kernel_index: int32 [128], P('band'), may hold values from 0 to 15
Outputs:
- image_new: float32 [128, 512, 512], P('band', 'row')
- vector_new: float32 [2, 128, 512, 512], P(None, 'band', 'row')
- grad_new: float32 [2, 128, 512, 512], P(None, 'band', 'row')
- sym_new: float32 [3, 128, 512, 512], P(None, 'band', 'row')
- data_new: float32 [128, 512, 512], P('band', 'row')
All inputs are finite; a program needn't handle non-finite values.
Results may differ from a plain program's by a relative error of at most 0.00007.
Values sent between devices are 32-bit elements; how exact they have to be, the bound alone decides.
A program may use at most 128 MiB of HBM per device.

v0:
```python
import jax
import jax.numpy as jnp
from jax import lax
from jax.sharding import PartitionSpec as P

STEP_PRIMAL = 0.25
STEP_DUAL = 0.25
FIDELITY = 2.0
BOUND_FIRST = 16.0
BOUND_SECOND = 24.0


def from_behind(value, axis, steps):
    count = lax.axis_size(axis)
    first, last = (max(0, -steps), min(count, count - steps))
    return lax.ppermute(value, axis, [(source, source + steps) for source in range(first, last)])


def with_halo(block, sides, width):
    for axis, dim in sides:
        count = lax.axis_size(axis)
        forward = [(i, i + 1) for i in range(count - 1)]
        backward = [(target, source) for source, target in forward]
        low = lax.ppermute(
            lax.slice_in_dim(block, block.shape[dim] - width, None, axis=dim), axis, forward
        )
        high = lax.ppermute(lax.slice_in_dim(block, 0, width, axis=dim), axis, backward)
        block = jnp.concatenate([low, block, high], axis=dim)
    return block


def blur_rows(extended, kernel):
    radius = kernel.shape[1] // 2
    result = lax.conv_general_dilated(
        extended[None],
        kernel[:, None],
        (1, 1),
        ((0, 0), (radius, radius)),
        dimension_numbers=("NCHW", "OIHW", "NCHW"),
        feature_group_count=extended.shape[0],
        precision=lax.Precision.HIGHEST,
    )
    return result[0]


def row_forward(field, following):
    return jnp.concatenate([field[:, 1:], following], 1) - field


def row_adjoint(field, previous):
    return jnp.concatenate([previous, field[:, :-1]], 1) - field


def column_forward(field):
    return jnp.concatenate([field[:, :, 1:], jnp.zeros_like(field[:, :, :1])], 2) - field


def column_adjoint(field):
    return jnp.concatenate([jnp.zeros_like(field[:, :, :1]), field[:, :, :-1]], 2) - field


def body(observed, image, vector_field, dual_grad, dual_sym, dual_data, kernels, kernel_index):
    band_count, row_count, col_count = image.shape
    radius = kernels.shape[1] // 2
    one_hot = (
        kernel_index[:, None] == jnp.arange(kernels.shape[0], dtype=jnp.int32)[None, :]
    ).astype(jnp.float32)
    weights = jnp.dot(
        one_hot, kernels.reshape(kernels.shape[0], -1), precision=lax.Precision.HIGHEST
    ).reshape(band_count, kernels.shape[1], kernels.shape[2])
    flipped = weights[:, ::-1, ::-1]
    last_rows = jnp.stack([dual_grad[0][:, -1:], dual_sym[0][:, -1:], dual_sym[2][:, -1:]])
    before = from_behind(last_rows, "row", 1)
    residual_rim = with_halo(dual_data, (("row", 1),), radius)
    adjoint_blur = blur_rows(residual_rim, flipped)
    image_new = image - STEP_PRIMAL * (
        adjoint_blur + row_adjoint(dual_grad[0], before[0]) + column_adjoint(dual_grad[1])
    )
    extrapolated = 2.0 * image_new - image
    vector_first = vector_field[0] - STEP_PRIMAL * (
        row_adjoint(dual_sym[0], before[1]) + column_adjoint(dual_sym[2]) - dual_grad[0]
    )
    vector_second = vector_field[1] - STEP_PRIMAL * (
        column_adjoint(dual_sym[1]) + row_adjoint(dual_sym[2], before[2]) - dual_grad[1]
    )
    vector_new = jnp.stack([vector_first, vector_second])
    vector_bar = 2.0 * vector_new - vector_field
    next_rows = from_behind(vector_bar[:, :, :1], "row", -1)
    bar_rim = with_halo(extrapolated, (("row", 1),), radius)
    bar_following = bar_rim[:, radius + 1 : radius + row_count + 1]
    blurred = blur_rows(bar_rim, weights)
    data_new = (dual_data + STEP_DUAL * (blurred - observed)) / (1.0 + STEP_DUAL / FIDELITY)
    grad_first = dual_grad[0] + STEP_DUAL * (bar_following - extrapolated - vector_bar[0])
    grad_second = dual_grad[1] + STEP_DUAL * (column_forward(extrapolated) - vector_bar[1])
    sym_first = dual_sym[0] + STEP_DUAL * row_forward(vector_bar[0], next_rows[0])
    sym_second = dual_sym[1] + STEP_DUAL * column_forward(vector_bar[1])
    sym_cross = dual_sym[2] + STEP_DUAL * 0.5 * (
        column_forward(vector_bar[0]) + row_forward(vector_bar[1], next_rows[1])
    )
    local_grad = jnp.sum(grad_first * grad_first + grad_second * grad_second, axis=0)
    local_sym = jnp.sum(
        sym_first * sym_first + sym_second * sym_second + 2.0 * sym_cross * sym_cross, axis=0
    )
    total_grad, total_sym = lax.psum((local_grad, local_sym), "band")
    scale_grad = 1.0 / jnp.maximum(1.0, jnp.sqrt(total_grad) / BOUND_FIRST)
    scale_sym = 1.0 / jnp.maximum(1.0, jnp.sqrt(total_sym) / BOUND_SECOND)
    grad_new = jnp.stack([grad_first, grad_second]) * scale_grad
    sym_new = jnp.stack([sym_first, sym_second, sym_cross]) * scale_sym
    return (image_new, vector_new, grad_new, sym_new, data_new)


def solution(mesh):
    placed = (
        P("band", "row", None),
        P("band", "row", None),
        P(None, "band", "row", None),
        P(None, "band", "row", None),
        P(None, "band", "row", None),
        P("band", "row", None),
        P(),
        P("band"),
    )
    return jax.shard_map(
        body,
        mesh=mesh,
        in_specs=placed,
        out_specs=(
            P("band", "row", None),
            P(None, "band", "row", None),
            P(None, "band", "row", None),
            P(None, "band", "row", None),
            P("band", "row", None),
        ),
        check_vma=False,
    )
```

profile of v0, /device:TPU:25, one launch (start us, length us, event | category | flops | bytes accessed | tf_op | source)
XLA Modules:
  0.0 373.4 jit_solution(6012682308851412032)
XLA Ops:
  13.7 3.1 collective-permute-start.2
  17.7 3.1 collective-permute-start
  20.8 5.2 %collective-permute-start.1 = (f32[16,7,512]{2,1,0:T(8,128)}, f32[16,7,512]{2,1,0:T(8,128)}, u32[]{:S(2)}, u32[]{:S(2)}) collective-permute-start(f32[16,7,512]{2,1,0:T(8,128)} %get-tuple-element.48), channel_id=1, source_target_pairs={{1,0},{2,1},{3,2},{4,3},{5,4},{6,5},{7,6},{8,7},{9,8},{10,9},{11,1... | collective-permute-start | bytes 688136 | tf_op jit(solution)/shard_map/ppermute | solution.py:27
  27.2 1.9 slice.166
  29.0 1.9 slice.162
  40.1 5.1 %copy.73 = f32[16,30,1,8,66]{0,3,4,1,2:T(8,128)} copy(f32[16,30,1,8,66]{4,3,1,0,2:T(8,128)S(1)} %reshape.48) | data formatting | bytes 2027520 | tf_op jit(solution)/shard_map/conv_general_dilated | solution.py:34
  46.8 8.3 %fusion.76 = f32[16,30,8,80]{0,2,3,1:T(8,128)} fusion(f32[16,30,1,7,14]{0,3,4,1,2:T(8,128)S(1)} %slice.156, f32[16,30,1,8,66]{0,3,4,1,2:T(8,128)} %copy.73), kind=kLoop, calls=%fused_computation.5.clone.clone.clone.clone | loop fusion | flops 921600 | bytes 2430720 | tf_op jit(solution)/shard_map/conv_general_dilated | solution.py:34
  55.2 87.6 %broadcast_select_fusion.1 = f32[16,8,66,16]{3,1,2,0:T(8,128)} fusion(pred[8,66]{0,1:T(8,128)(4,1)S(1)} %copy-done.36, f32[16,1,15,15]{0,1,3,2:T(1,128)S(1)} %copy.75, f32[16,30,8,80]{0,2,3,1:T(8,128)} %fusion.76), kind=kOutput, calls=%fused_computation.16 | convolution fusion | flops 365088768 | bytes 1784400 | tf_op jit(solution)/shard_map/conv_general_dilated | solution.py:34
  142.8 4.0 %copy.76 = f32[16,8,66,16]{2,1,3,0:T(8,128)} copy(f32[16,8,66,16]{3,1,2,0:T(8,128)} %broadcast_select_fusion.1) | data formatting | bytes 1081344 | tf_op jit(solution)/shard_map/conv_general_dilated | solution.py:34
  146.8 2.4 reshape.30
  149.3 4.8 %fusion.31 = (f32[1,16,16,512]{3,1,2,0:T(8,128)S(1)}, f32[1,16,16,512]{3,1,2,0:T(8,128)S(1)}, f32[16,16,512]{2,0,1:T(8,128)S(1)}, f32[16,16,512]{2,0,1:T(8,128)S(1)}) fusion(f32[2,16,16,512]{3,1,2,0:T(8,128)} %copy.82, f32[16,15,512]{2,0,1:T(8,128)} %slice.166, f32[16,1,512]{2,0,1:T(8,128)S(1)} %copy-done.29, f32[16,16,511]{2,0,1:T(8,128)S(1)} %bitcast.178, ...), kind=kLoop, calls=%fused_computation.42 | loop fusion | flops 3014656 | bytes 9958400 | tf_op jit(solution)/shard_map/stack | solution.py:86
  155.1 2.2 collective-permute-start.4
  158.5 2.9 collective-permute-start.3
  161.4 2.4 collective-permute-start.5
  168.1 3.0 fusion.19
  173.0 5.2 %copy.88 = f32[16,30,1,8,66]{0,3,4,1,2:T(8,128)} copy(f32[16,30,1,8,66]{4,3,0,1,2:T(8,128)S(1)} %reshape.33) | data formatting | bytes 2027520 | tf_op jit(solution)/shard_map/conv_general_dilated | solution.py:34
  179.9 8.3 %fusion.74 = f32[16,30,8,80]{0,2,3,1:T(8,128)} fusion(f32[16,30,1,7,14]{0,3,4,1,2:T(8,128)S(1)} %slice.184, f32[16,30,1,8,66]{0,3,4,1,2:T(8,128)} %copy.88), kind=kLoop, calls=%fused_computation.1.clone.clone.clone.clone.1 | loop fusion | flops 921600 | bytes 2430720 | tf_op jit(solution)/shard_map/conv_general_dilated | solution.py:34
  188.2 87.4 %broadcast_select_fusion = f32[16,8,66,16]{3,1,2,0:T(8,128)} fusion(pred[8,66]{0,1:T(8,128)(4,1)S(1)} %copy-done.36, f32[16,1,15,15]{0,1,3,2:T(1,128)S(1)} %copy-done.33, f32[16,30,8,80]{0,2,3,1:T(8,128)} %fusion.74), kind=kOutput, calls=%fused_computation.15 | convolution fusion | flops 365088768 | bytes 1784400 | tf_op jit(solution)/shard_map/conv_general_dilated | solution.py:34
  275.6 4.0 %copy.90 = f32[16,8,66,16]{2,1,3,0:T(8,128)} copy(f32[16,8,66,16]{3,1,2,0:T(8,128)} %broadcast_select_fusion) | data formatting | bytes 1081344 | tf_op jit(solution)/shard_map/conv_general_dilated | solution.py:34
  279.7 2.5 reshape.37
  282.2 3.5 add_reduce_fusion
  285.7 2.0 fusion.23
  288.8 71.4 %all-reduce.9.cloned.1.call-done = (f32[16,512]{1,0:T(8,128)}, f32[16,512]{1,0:T(8,128)}) async-done(((f32[16,512]{1,0:T(8,128)}, f32[16,512]{1,0:T(8,128)}), (f32[16,512]{1,0:T(8,128)}, f32[16,512]{1,0:T(8,128)})) %all-reduce.9.cloned.1.call-update) | async-done | bytes 65552 | tf_op jit(solution)/shard_map/psum | solution.py:104
  362.5 2.1 copy.96
  (131 shorter events, 34.4 us)
Async XLA Ops:
  7.2 9.7 %copy-start.18 = (f32[16,16,512]{2,1,0:T(8,128)S(1)}, f32[16,16,512]{2,1,0:T(8,128)}, u32[]{:S(2)}) copy-start(f32[16,16,512]{2,1,0:T(8,128)} %param.13) | copy-start | bytes 1572868
  7.2 18.8 %copy-start.32 = (f32[16,15,15]{2,0,1:T(8,128)S(1)}, f32[16,15,15]{2,0,1:T(8,128)}, u32[]{:S(2)}) copy-start(f32[16,15,15]{2,0,1:T(8,128)} %param.14) | copy-start | bytes 43204
  7.2 353.0 %all-reduce.9.cloned.1.call-start = ((), (), s32[]{:S(2)}) async-start(), calls=%async_computation | async-start | bytes 131072 | tf_op jit(solution)/shard_map/psum | solution.py:104
  8.9 22.6 %copy-start.12 = (f32[1,16,16,512]{3,2,1,0:T(8,128)}, f32[1,16,16,512]{3,2,1,0:T(8,128)S(1)}, u32[]{:S(2)}) copy-start(f32[1,16,16,512]{3,2,1,0:T(8,128)S(1)} %get-tuple-element.32) | copy-start | bytes 1572868
  8.9 17.3 %copy-start.35 = (s32[16]{0:T(128)S(1)}, s32[16]{0:T(128)}, u32[]{:S(2)}) copy-start(s32[16]{0:T(128)} %param.15) | copy-start | bytes 196
  10.3 21.2 %copy-start.16 = (f32[16,16,512]{2,0,1:T(8,128)}, f32[16,16,512]{2,0,1:T(8,128)S(1)}, u32[]{:S(2)}) copy-start(f32[16,16,512]{2,0,1:T(8,128)S(1)} %get-tuple-element.55) | copy-start | bytes 1572868
  11.2 22.5 %copy-start.9 = (f32[1,16,16,512]{3,2,1,0:T(8,128)}, f32[1,16,16,512]{3,2,1,0:T(8,128)S(1)}, u32[]{:S(2)}) copy-start(f32[1,16,16,512]{3,2,1,0:T(8,128)S(1)} %get-tuple-element.42) | copy-start | bytes 1572868
  11.9 21.8 %copy-start.20 = (f32[2,16,16,512]{3,2,1,0:T(8,128)S(1)}, f32[2,16,16,512]{3,2,1,0:T(8,128)}, u32[]{:S(2)}) copy-start(f32[2,16,16,512]{3,2,1,0:T(8,128)} %param.10) | copy-start | bytes 3145732
  13.7 22.4 %collective-permute-start.2 = (f32[3,16,1,512]{3,1,2,0:T(8,128)}, f32[3,16,1,512]{3,1,2,0:T(8,128)}, u32[]{:S(2)}, u32[]{:S(2)}) collective-permute-start(f32[3,16,1,512]{3,1,2,0:T(8,128)} %pad_maximum_fusion.2), channel_id=1, source_target_pairs={{0,1},{1,2},{2,3},{3,4},{4,5},{5,6},{6,7},{7,8},{8,9},{9,10},{10,1... | collective-permute-start | bytes 294920 | tf_op jit(solution)/shard_map/ppermute | solution.py:16
  17.7 19.9 %collective-permute-start = (f32[16,7,512]{2,1,0:T(8,128)}, f32[16,7,512]{2,1,0:T(8,128)}, u32[]{:S(2)}, u32[]{:S(2)}) collective-permute-start(f32[16,7,512]{2,1,0:T(8,128)} %get-tuple-element.47), channel_id=1, source_target_pairs={{0,1},{1,2},{2,3},{3,4},{4,5},{5,6},{6,7},{7,8},{8,9},{9,10},{10,1... | collective-permute-start | bytes 688136 | tf_op jit(solution)/shard_map/ppermute | solution.py:24
  20.8 16.8 %collective-permute-start.1 = (f32[16,7,512]{2,1,0:T(8,128)}, f32[16,7,512]{2,1,0:T(8,128)}, u32[]{:S(2)}, u32[]{:S(2)}) collective-permute-start(f32[16,7,512]{2,1,0:T(8,128)} %get-tuple-element.48), channel_id=1, source_target_pairs={{1,0},{2,1},{3,2},{4,3},{5,4},{6,5},{7,6},{8,7},{9,8},{10,9},{11,1... | collective-permute-start | bytes 688136 | tf_op jit(solution)/shard_map/ppermute | solution.py:27
  46.8 8.3 %copy-start.36 = (pred[8,66]{0,1:T(8,128)(4,1)S(1)}, pred[8,66]{0,1:T(8,128)(4,1)}, u32[]{:S(2)}) copy-start(pred[8,66]{0,1:T(8,128)(4,1)} %constant.51) | copy-start | bytes 1588
  154.1 17.1 %copy-start.4 = (f32[16,16,512]{2,0,1:T(8,128)}, f32[16,16,512]{2,0,1:T(8,128)S(1)}, u32[]{:S(2)}) copy-start(f32[16,16,512]{2,0,1:T(8,128)S(1)} %get-tuple-element.35) | copy-start | bytes 1572868
  154.9 13.1 %copy-start = (f32[2,16,16,512]{3,1,2,0:T(8,128)}, f32[2,16,16,512]{3,1,2,0:T(8,128)S(1)}, u32[]{:S(2)}) copy-start(f32[2,16,16,512]{3,1,2,0:T(8,128)S(1)} %get-tuple-element.39) | copy-start | bytes 3145732
  155.1 11.4 %collective-permute-start.4 = (f32[2,16,1,512]{3,1,2,0:T(8,128)S(1)}, f32[2,16,1,512]{3,1,2,0:T(8,128)S(1)}, u32[]{:S(2)}, u32[]{:S(2)}) collective-permute-start(f32[2,16,1,512]{3,1,2,0:T(8,128)S(1)} %slice.177), channel_id=1, source_target_pairs={{1,0},{2,1},{3,2},{4,3},{5,4},{6,5},{7,6},{8,7},{9,8},{10,9},{11,1... | collective-permute-start | bytes 196616 | tf_op jit(solution)/shard_map/ppermute | solution.py:16
  158.5 12.5 %collective-permute-start.3 = (f32[16,7,512]{2,0,1:T(8,128)S(1)}, f32[16,7,512]{2,0,1:T(8,128)S(1)}, u32[]{:S(2)}, u32[]{:S(2)}) collective-permute-start(f32[16,7,512]{2,0,1:T(8,128)S(1)} %get-tuple-element.44), channel_id=1, source_target_pairs={{1,0},{2,1},{3,2},{4,3},{5,4},{6,5},{7,6},{8,7},{9,8},{10,9},{11,1... | collective-permute-start | bytes 688136 | tf_op jit(solution)/shard_map/ppermute | solution.py:27
  161.4 9.8 %collective-permute-start.5 = (f32[16,7,512]{2,0,1:T(8,128)S(1)}, f32[16,7,512]{2,0,1:T(8,128)S(1)}, u32[]{:S(2)}, u32[]{:S(2)}) collective-permute-start(f32[16,7,512]{2,0,1:T(8,128)S(1)} %get-tuple-element.43), channel_id=1, source_target_pairs={{0,1},{1,2},{2,3},{3,4},{4,5},{5,6},{6,7},{7,8},{8,9},{9,10},{10,1... | collective-permute-start | bytes 688136 | tf_op jit(solution)/shard_map/ppermute | solution.py:24
  179.8 8.4 %copy-start.33 = (f32[16,1,15,15]{0,1,3,2:T(1,128)S(1)}, f32[16,1,15,15]{0,1,3,2:T(1,128)}, u32[]{:S(2)}) copy-start(f32[16,1,15,15]{0,1,3,2:T(1,128)} %copy.89) | copy-start | bytes 43204
  275.6 6.5 %copy-start.1 = (f32[2,16,16,512]{3,1,2,0:T(8,128)S(1)}, f32[2,16,16,512]{3,1,2,0:T(8,128)}, u32[]{:S(2)}) copy-start(f32[2,16,16,512]{3,1,2,0:T(8,128)} %copy-done) | copy-start | bytes 3145732
  275.6 6.5 %copy-start.5 = (f32[16,16,512]{2,0,1:T(8,128)S(1)}, f32[16,16,512]{2,0,1:T(8,128)}, u32[]{:S(2)}) copy-start(f32[16,16,512]{2,0,1:T(8,128)} %copy-done.4) | copy-start | bytes 1572868
  275.6 6.5 %copy-start.8 = (f32[1,16,16,512]{3,2,1,0:T(8,128)S(1)}, f32[1,16,16,512]{3,2,1,0:T(8,128)}, u32[]{:S(2)}) copy-start(f32[1,16,16,512]{3,2,1,0:T(8,128)} %copy-done.6) | copy-start | bytes 1572868
  275.6 6.5 %copy-start.11 = (f32[1,16,16,512]{3,2,1,0:T(8,128)S(1)}, f32[1,16,16,512]{3,2,1,0:T(8,128)}, u32[]{:S(2)}) copy-start(f32[1,16,16,512]{3,2,1,0:T(8,128)} %copy-done.9) | copy-start | bytes 1572868
  285.7 78.9 %copy-start.22 = (f32[16,16,512]{2,0,1:T(8,128)S(1)}, f32[16,16,512]{2,0,1:T(8,128)}, u32[]{:S(2)}) copy-start(f32[16,16,512]{2,0,1:T(8,128)} %get-tuple-element.25) | copy-start | bytes 1572868
  285.7 78.9 %copy-start.23 = (f32[16,16,512]{2,0,1:T(8,128)S(1)}, f32[16,16,512]{2,0,1:T(8,128)}, u32[]{:S(2)}) copy-start(f32[16,16,512]{2,0,1:T(8,128)} %get-tuple-element.26) | copy-start | bytes 1572868
  (20 other events, 91.3 us)
Sparse Core Ops, SparseCore 0:
  285.8 74.3 all-reduce.8
where the time goes:
time: 380 us; the launch traced here: 373 us
  matrix products  175 us (46%)
  waiting for transfers between devices  71.6 us (19%)
  local copies, waits for them, and re-layouts  56.5 us (15%)
  other arithmetic  36.4 us (10%)
  starting transfers between devices  18.9 us (5%)
  between operations  14.9 us (4%)
    conv_general_dilated x2, matrix products, blur_rows(): lax.conv_general_dilated(extended[None], kernel[:, None], (1, 1), ((0, 0)...  175 us
    psum x1, waiting for transfers between devices, body(): total_grad, total_sym = lax.psum((local_grad, local_sym), 'band')  71.4 us
    conv_general_dilated x10, local copies, waits for them, and re-layouts, blur_rows(): lax.conv_general_dilated(extended[None], kernel[:, None], (1, 1), ((0, 0)...  28.3 us
    conv_general_dilated x2, other arithmetic, blur_rows(): lax.conv_general_dilated(extended[None], kernel[:, None], (1, 1), ((0, 0)...  16.7 us
    unnamed x84, local copies, waits for them, and re-layouts  15.2 us
    ppermute x2, starting transfers between devices, with_halo(): lax.ppermute(lax.slice_in_dim(block, 0, width, axis=dim), axis, backward)  8.07 us
  transfers between devices with their start and end apart: 7, of which 2 were waited for; matrix products, arithmetic and copies ran while one was open for 6% of the time, Pallas kernels for 0%

commit v1 on v0

v1 whole, which is shorter than its diff:
```python
import functools

import jax
import jax.numpy as jnp
from jax import lax
from jax.experimental import pallas as pl
from jax.experimental.pallas import tpu as pltpu
from jax.sharding import PartitionSpec as P

FIDELITY = 2.0
STEP_DUAL = 0.25
BOUND_FIRST = 16.0
BOUND_SECOND = 24.0
MESH = pl.DeviceIdType.MESH
F32 = jnp.float32
BF16 = jnp.bfloat16
CHUNK = 4


def split(value):
    high = value.astype(BF16)
    return high, (value - high.astype(F32)).astype(BF16)


def toeplitz_scatter(table_ref, index, out_ref, band):
    lane = lax.broadcasted_iota(jnp.int32, (8, 128), 1)
    first = lane % 32 < 16
    for a in range(4):
        row = jnp.broadcast_to(table_ref[index, pl.ds(a, 1), :], (8, 128))
        groups = []
        for base in (0, 8, -8, 16):
            moved = pltpu.roll(row, (base - 7) % 128, 1, stride=1, stride_axis=0)
            groups.append(jnp.where(first, moved, pltpu.roll(moved, 16, 1)))
        high, low = split(jnp.concatenate(groups, 0))
        out_ref[band, pl.ds(32 * a, 32), pl.ds(0, 128)] = high
        out_ref[band, pl.ds(32 * a, 32), pl.ds(128, 128)] = low


def toeplitz_gather(table_ref, index, out_ref, band):
    lane = lax.broadcasted_iota(jnp.int32, (8, 128), 1) % 32
    for a in range(4):
        row = jnp.broadcast_to(table_ref[index, pl.ds(a, 1), :], (8, 128))
        groups = []
        for base in (0, 8):
            own = pltpu.roll(row, (base - 7) % 128, 1, stride=1, stride_axis=0)
            above = pltpu.roll(row, base + 17, 1, stride=1, stride_axis=0)
            below = pltpu.roll(row, base + 1, 1, stride=1, stride_axis=0)
            groups.append(jnp.where(lane < 16, own, jnp.where(lane < 24, above, below)))
        high, low = split(jnp.concatenate(groups, 0))
        out_ref[band, pl.ds(16 * a, 16), pl.ds(0, 128)] = high
        out_ref[band, pl.ds(16 * a, 16), pl.ds(128, 128)] = high
        out_ref[band, pl.ds(16 * a, 16), pl.ds(256, 128)] = low


def padded_shifts(field):
    rows, cols = field.shape
    wide = jnp.concatenate([field, jnp.zeros((rows, 128), F32)], 1)
    return [split(wide if b == 3 else pltpu.roll(wide, 3 - b, 1)) for b in range(4)]


def gather_shifts(product, rows, cols):
    width = product.shape[1]
    total = product[rows : 2 * rows]
    for a in (0, 2, 3):
        total = total + pltpu.roll(product[a * rows : (a + 1) * rows], (4 - 4 * a) % width, 1)
    return total[:, :cols]


def column_before(field):
    lane = lax.broadcasted_iota(jnp.int32, field.shape, 1)
    return jnp.where(lane == 0, 0.0, pltpu.roll(field, 1, 1))


def column_after(field):
    cols = field.shape[1]
    lane = lax.broadcasted_iota(jnp.int32, field.shape, 1)
    return jnp.where(lane == cols - 1, 0.0, pltpu.roll(field, cols - 1, 1))


def row_before(field, first):
    line = lax.broadcasted_iota(jnp.int32, field.shape, 0)
    return jnp.where(line == 0, first, pltpu.roll(field, 1, 0))


def row_after(field, last):
    rows = field.shape[0]
    line = lax.broadcasted_iota(jnp.int32, field.shape, 0)
    return jnp.where(line == rows - 1, last, pltpu.roll(field, rows - 1, 0))


def kernel(
    bands, rows, cols, band_axis, row_axis,
    index_ref, adjoint_ref, forward_ref,
    observed_hbm, image_hbm, vector_hbm, grad_hbm, sym_hbm, data_hbm,
    image_out, vector_out, grad_out, sym_out, data_out,
    obs, img, vec, grad, sym, data, bar, scatter_w, gather_w,
    line_up, line_dn, line_from_dn, line_from_up,
    near_up, near_dn, near_from_dn, near_from_up,
    far_up, far_dn, far_from_dn, far_from_up,
    part_out, part_in, scale_buf,
    in_sem, out_sem, line_send, line_recv, near_send, near_recv, far_send, far_recv,
    part_send, part_recv, scale_send, scale_recv,
):
    me_row, me_band = lax.axis_index("row"), lax.axis_index("band")
    up = lax.rem(me_row + row_axis - 1, row_axis)
    down = lax.rem(me_row + 1, row_axis)
    peers = [lax.rem(me_band + k, band_axis) for k in range(1, band_axis)]
    not_top = jnp.where(me_row > 0, 1.0, 0.0).astype(F32)
    not_end = jnp.where(me_row < row_axis - 1, 1.0, 0.0).astype(F32)
    chunks = bands // CHUNK

    barrier = pltpu.get_barrier_semaphore()
    for target in (up, down):
        pl.semaphore_signal(barrier, inc=1, device_id={"row": target}, device_id_type=MESH)
    for target in peers:
        pl.semaphore_signal(barrier, inc=1, device_id={"band": target}, device_id_type=MESH)

    loads = [
        pltpu.make_async_copy(source, target, in_sem.at[k])
        for k, (source, target) in enumerate(
            ((sym_hbm, sym), (vector_hbm, vec), (grad_hbm, grad), (data_hbm, data), (image_hbm, img), (observed_hbm, obs))
        )
    ]
    for load in loads:
        load.start()

    def to_row(source, target, send, recv, which):
        return pltpu.make_async_remote_copy(
            src_ref=source, dst_ref=target, send_sem=send, recv_sem=recv,
            device_id={"row": which}, device_id_type=MESH,
        )

    def to_band(source, target, send, recv, which):
        return pltpu.make_async_remote_copy(
            src_ref=source, dst_ref=target, send_sem=send, recv_sem=recv,
            device_id={"band": which}, device_id_type=MESH,
        )

    line_copies = (
        to_row(line_up, line_from_dn, line_send.at[0], line_recv.at[0], up),
        to_row(line_dn, line_from_up, line_send.at[1], line_recv.at[1], down),
    )

    def near_copies(c):
        return (
            to_row(near_up.at[c], near_from_dn.at[c], near_send.at[0, c], near_recv.at[0, c], up),
            to_row(near_dn.at[c], near_from_up.at[c], near_send.at[1, c], near_recv.at[1, c], down),
        )

    def far_copies(c):
        body = pl.ds(8, 6 * CHUNK)
        return (
            to_row(far_up.at[c, body], far_from_dn.at[c, body], far_send.at[0, c], far_recv.at[0, c], up),
            to_row(far_dn.at[c, body], far_from_up.at[c, body], far_send.at[1, c], far_recv.at[1, c], down),
        )

    def scatter_weights(band, carry):
        toeplitz_scatter(adjoint_ref, index_ref[band], scatter_w, band)
        return carry

    lax.fori_loop(0, bands, scatter_weights, 0)

    for load in loads[:3]:
        load.wait()

    def pack_lines(band, carry):
        top = pl.ds(0, 1)
        cross, p0, p1 = sym[2, band, top, :], grad[0, band, top, :], grad[1, band, top, :]
        q0, q1 = sym[0, band, top, :], sym[1, band, top, :]
        line_up[0, band] = vec[0, band, top, :] + 0.5 * (q0 - (column_before(cross) - cross) + p0)
        line_up[1, band] = vec[1, band, top, :] + 0.5 * (cross - (column_before(q1) - q1) + p1)
        line_dn[0, band] = sym[0, band, pl.ds(rows - 1, 1), :]
        line_dn[1, band] = sym[2, band, pl.ds(rows - 1, 1), :]
        return carry

    lax.fori_loop(0, bands, pack_lines, 0)
    pl.semaphore_wait(barrier, 2 + len(peers))
    for copy in line_copies:
        copy.start()

    for load in loads[3:5]:
        load.wait()
    tile_line = lax.broadcasted_iota(jnp.int32, (8, cols), 0)

    def adjoint(c, carry):
        for k in range(CHUNK):
            band = c * CHUNK + k
            parts = [part for pair in padded_shifts(data[band]) for part in pair]
            stacked = jnp.concatenate(parts + parts, 0)
            product = jnp.dot(scatter_w[band], stacked, preferred_element_type=F32)
            total = gather_shifts(product, 2 * rows, cols)
            p0, p1 = grad[0, band], grad[1, band]
            own = img[band] + total[:rows] - 0.5 * (row_before(p0, 0.0) - p0 + column_before(p1) - p1)
            bar[band] = own
            above, below = total[rows : rows + 8], total[rows + 8 : rows + 16]
            near_up[c, k] = jnp.where(tile_line == 0, own[:8], above)
            below = below - jnp.where(tile_line == 0, 0.5 * pltpu.roll(p0[8:], 1, 0), 0.0)
            near_dn[c, k] = jnp.where(tile_line == 7, own[8:], below)
            far_up[c, pl.ds(8 + 6 * k, 6), :] = own[1:7]
            far_dn[c, pl.ds(8 + 6 * k, 6), :] = own[9:15]
        for copy in near_copies(c):
            copy.start()
        return carry

    lax.fori_loop(0, chunks, adjoint, 0)

    def start_far(c, carry):
        for copy in far_copies(c):
            copy.start()
        return carry

    lax.fori_loop(0, chunks, start_far, 0)

    def gather_weights(band, carry):
        toeplitz_gather(forward_ref, index_ref[band], gather_w, band)
        return carry

    lax.fori_loop(0, bands, gather_weights, 0)

    for copy in line_copies:
        copy.wait_recv()

    def symmetric(band, norm):
        q0, q1, q2 = sym[0, band], sym[1, band], sym[2, band]
        p0, p1 = grad[0, band], grad[1, band]
        v0, v1 = vec[0, band], vec[1, band]
        prev0, prev2 = not_top * line_from_up[0, band], not_top * line_from_up[1, band]
        step0 = 0.25 * (row_before(q0, prev0) - q0 + column_before(q2) - q2 - p0)
        step1 = 0.25 * (column_before(q1) - q1 + row_before(q2, prev2) - q2 - p1)
        vec[0, band] = v0 - step0
        vec[1, band] = v1 - step1
        bar0, bar1 = v0 - 2.0 * step0, v1 - 2.0 * step1
        end = pl.ds(rows - 1, 1)
        next0 = not_end * (line_from_dn[0, band] - 0.5 * sym[0, band, end, :])
        next1 = not_end * (line_from_dn[1, band] - 0.5 * sym[2, band, end, :])
        new0 = q0 + 0.25 * (row_after(bar0, next0) - bar0)
        new1 = q1 + 0.25 * (column_after(bar1) - bar1)
        new2 = q2 + 0.125 * (column_after(bar0) - bar0 + row_after(bar1, next1) - bar1)
        sym[0, band] = new0
        sym[1, band] = new1
        sym[2, band] = new2
        grad[0, band] = p0 - 0.25 * bar0
        grad[1, band] = p1 - 0.25 * bar1
        return norm + (new0 * new0 + new1 * new1 + 2.0 * (new2 * new2))

    each = cols // 128 * (rows // 8) // band_axis

    def send_parts(which, norm):
        for piece in range(each * band_axis):
            half, tile = divmod(piece, cols // 128)
            part_out[which, piece // each, piece % each] = norm[8 * half : 8 * half + 8, 128 * tile : 128 * tile + 128]
        part_in[which, me_band] = part_out[which, me_band]
        for peer in peers:
            to_band(
                part_out.at[which, peer], part_in.at[which, me_band],
                part_send.at[which, peer], part_recv.at[which, me_band], peer,
            ).start()

    def send_scales(which, bound):
        for peer in peers:
            to_band(
                part_out.at[which, peer], part_in.at[which, peer],
                part_send.at[which, peer], part_recv.at[which, peer], peer,
            ).wait()
        total = part_in[which, 0]
        for source in range(1, band_axis):
            total = total + part_in[which, source]
        scale_buf[which, me_band] = 1.0 / jnp.maximum(1.0, jnp.sqrt(total) * (1.0 / bound))
        for peer in peers:
            to_band(
                scale_buf.at[which, me_band], scale_buf.at[which, me_band],
                scale_send.at[which, peer], scale_recv.at[which, me_band], peer,
            ).start()

    def wait_scales(which):
        for peer in peers:
            to_band(
                scale_buf.at[which, me_band], scale_buf.at[which, peer],
                scale_send.at[which, peer], scale_recv.at[which, peer], peer,
            ).wait()
        tiles = [scale_buf[which, piece // each, piece % each] for piece in range(each * band_axis)]
        wide = cols // 128
        return jnp.concatenate([jnp.concatenate(tiles[h * wide : h * wide + wide], 1) for h in range(rows // 8)], 0)

    norm_sym = lax.fori_loop(0, bands, symmetric, jnp.zeros((rows, cols), F32))
    send_parts(0, norm_sym)
    store_vec = pltpu.make_async_copy(vec, vector_out, out_sem.at[0])
    store_vec.start()

    def first_order(c, norm):
        for copy in near_copies(c):
            copy.wait_recv()
        for k in range(CHUNK):
            band = c * CHUNK + k
            part = bar[band]
            from_up, from_dn = near_from_up[c, k], near_from_dn[c, k]
            top = part[:8] + jnp.where(tile_line == 7, 0.0, not_top * from_up)
            end = part[8:] + jnp.where(tile_line == 0, 0.0, not_end * from_dn)
            own = jnp.concatenate([top, end], 0)
            bar[band] = own
            img[band] = 0.5 * (img[band] + own)
            following = not_end * (near_from_dn[c, k, pl.ds(0, 1), :] + near_dn[c, k, pl.ds(0, 1), :])
            new0 = grad[0, band] + 0.25 * (row_after(own, following) - own)
            new1 = grad[1, band] + 0.25 * (column_after(own) - own)
            grad[0, band] = new0
            grad[1, band] = new1
            norm = norm + (new0 * new0 + new1 * new1)
        return norm

    norm_grad = lax.fori_loop(0, chunks, first_order, jnp.zeros((rows, cols), F32))
    send_parts(1, norm_grad)
    store_img = pltpu.make_async_copy(img, image_out, out_sem.at[1])
    store_img.start()
    send_scales(0, BOUND_SECOND)
    loads[5].wait()

    def forward(c, carry):
        for copy in far_copies(c):
            copy.wait_recv()
        for k in range(CHUNK):
            band = c * CHUNK + k
            middle = (tile_line >= 1) & (tile_line <= 6)
            near = pl.ds(7 + 6 * k, 8)
            above = jnp.where(middle, far_from_up[c, near, :], near_from_up[c, k])
            above = not_top * jnp.where(tile_line == 0, 0.0, above + near_up[c, k])
            below = jnp.where(middle, far_from_dn[c, near, :], near_from_dn[c, k])
            below = not_end * jnp.where(tile_line == 7, 0.0, below + near_dn[c, k])
            pairs = padded_shifts(jnp.concatenate([bar[band], above, below], 0))
            highs, lows = [pair[0] for pair in pairs], [pair[1] for pair in pairs]
            stacked = jnp.concatenate(highs + lows + highs, 0)
            product = jnp.dot(gather_w[band], stacked, preferred_element_type=F32)
            blurred = gather_shifts(product, rows, cols)
            data[band] = (data[band] + (blurred - STEP_DUAL * obs[band])) * (1.0 / (1.0 + STEP_DUAL / FIDELITY))
        return carry

    lax.fori_loop(0, chunks, forward, 0)
    store_data = pltpu.make_async_copy(data, data_out, out_sem.at[2])
    store_data.start()

    send_scales(1, BOUND_FIRST)
    scale_sym = wait_scales(0)

    def scale_second(band, carry):
        for k in range(3):
            sym[k, band] = sym[k, band] * scale_sym
        return carry

    lax.fori_loop(0, bands, scale_second, 0)
    store_sym = pltpu.make_async_copy(sym, sym_out, out_sem.at[3])
    store_sym.start()

    scale_grad = wait_scales(1)

    def scale_first(band, carry):
        for k in range(2):
            grad[k, band] = grad[k, band] * scale_grad
        return carry

    lax.fori_loop(0, bands, scale_first, 0)
    store_grad = pltpu.make_async_copy(grad, grad_out, out_sem.at[4])
    store_grad.start()

    for copy in line_copies:
        copy.wait_send()

    def finish(c, carry):
        for copy in near_copies(c) + far_copies(c):
            copy.wait_send()
        return carry

    lax.fori_loop(0, chunks, finish, 0)
    for store in (store_vec, store_img, store_data, store_sym, store_grad):
        store.wait()


def spread(kernels, factor):
    count, size, _ = kernels.shape
    turned = jnp.pad(jnp.transpose(kernels, (0, 2, 1)), ((0, 0), (0, 16 - size), (0, 32 - size)))
    return (factor * turned).reshape(count, 4, 128)


def body(band_axis, row_axis, observed, image, vector_field, dual_grad, dual_sym, dual_data, kernels, kernel_index):
    bands, rows, cols = image.shape
    adjoint = spread(kernels[:, ::-1, ::-1], -0.5)
    forward = spread(kernels, STEP_DUAL)
    chunks = bands // CHUNK
    each = cols // 128 * (rows // 8) // band_axis
    vmem = pltpu.VMEM
    near, far = (chunks, CHUNK, 8, cols), (chunks, 16 + 6 * CHUNK, cols)
    line = (2, bands, 1, cols)
    parts = (2, band_axis, each, 8, 128)
    dma = pltpu.SemaphoreType.DMA
    anywhere = pl.BlockSpec(memory_space=pl.ANY)
    inside = pl.BlockSpec(memory_space=pltpu.VMEM)
    arrays = (observed, image, vector_field, dual_grad, dual_sym, dual_data)
    return pl.pallas_call(
        functools.partial(kernel, bands, rows, cols, band_axis, row_axis),
        out_shape=[
            jax.ShapeDtypeStruct(a.shape, F32) for a in (image, vector_field, dual_grad, dual_sym, dual_data)
        ],
        in_specs=[pl.BlockSpec(memory_space=pltpu.SMEM), inside, inside] + [anywhere] * 6,
        out_specs=[anywhere] * 5,
        scratch_shapes=[vmem(a.shape, F32) for a in arrays]
        + [vmem(image.shape, F32), vmem((bands, 8 * rows, 256), BF16), vmem((bands, 4 * rows, 384), BF16)]
        + [vmem(line, F32)] * 4
        + [vmem(near, F32)] * 4
        + [vmem(far, F32)] * 4
        + [vmem(parts, F32)] * 3
        + [dma((6,)), dma((5,)), dma((2,)), dma((2,))]
        + [dma((2, chunks))] * 4
        + [dma((2, band_axis))] * 4,
        compiler_params=pltpu.CompilerParams(
            collective_id=0, has_side_effects=True, vmem_limit_bytes=40 * 1024 * 1024
        ),
    )(kernel_index, adjoint, forward, *arrays)


def solution(mesh):
    placed = (
        P("band", "row", None),
        P("band", "row", None),
        P(None, "band", "row", None),
        P(None, "band", "row", None),
        P(None, "band", "row", None),
        P("band", "row", None),
        P(),
        P("band"),
    )
    return jax.shard_map(
        functools.partial(body, mesh.shape["band"], mesh.shape["row"]),
        mesh=mesh,
        in_specs=placed,
        out_specs=(
            P("band", "row", None),
            P(None, "band", "row", None),
            P(None, "band", "row", None),
            P(None, "band", "row", None),
            P("band", "row", None),
        ),
        check_vma=False,
    )
```

time: 380 us -> 49 us (0.13)
  the two profiles are of different devices: /device:TPU:25 before, /device:TPU:1 now
where the time goes in v1:
time: 49 us; the launch traced here: 48.6 us
  Pallas kernels  35.3 us (72%)
  local copies, waits for them, and re-layouts  12.6 us (26%)
  between operations  0.7 us (1%)
    pallas_call x1, Pallas kernels, body(): pl.pallas_call(functools.partial(kernel, bands, rows, cols, band_axis, ro...  35.3 us
    unnamed x20, local copies, waits for them, and re-layouts  12.3 us

profile of v1, /device:TPU:1, one launch (start us, length us, event | category | flops | bytes accessed | tf_op | source)
XLA Modules:
  0.0 48.6 jit_solution(15806926944616107954)
XLA Ops:
  0.6 0.0 copy-start.1
  0.6 1.2 %copy.15 = f32[16,15,15]{1,2,0:T(8,128)S(1)} copy(f32[16,15,15]{2,0,1:T(8,128)} %param.14) | data formatting | bytes 28800 | tf_op args[6]
  1.9 0.1 reshape.17.forward_ref
  2.0 0.2 rev.3
  2.2 0.1 reshape.16.adjoint_ref
  2.3 0.0 copy-done.1
  2.3 0.0 copy-start
  2.3 1.4 %copy-done = f32[3,16,16,512]{3,2,1,0:T(8,128)S(1)} copy-done((f32[3,16,16,512]{3,2,1,0:T(8,128)S(1)}, f32[3,16,16,512]{3,2,1,0:T(8,128)}, u32[]{:S(2)}) %copy-start) | copy-done | bytes 1572888
  3.7 0.0 copy-start.2
  3.7 1.2 %copy-done.2 = f32[2,16,16,512]{3,2,1,0:T(8,128)S(1)} copy-done((f32[2,16,16,512]{3,2,1,0:T(8,128)S(1)}, f32[2,16,16,512]{3,2,1,0:T(8,128)}, u32[]{:S(2)}) %copy-start.2) | copy-done | bytes 1048600
  4.9 0.0 copy-start.3
  4.9 1.0 %copy-done.3 = f32[16,16,512]{2,1,0:T(8,128)S(1)} copy-done((f32[16,16,512]{2,1,0:T(8,128)S(1)}, f32[16,16,512]{2,1,0:T(8,128)}, u32[]{:S(2)}) %copy-start.3) | copy-done | bytes 524312
  5.9 0.0 copy-start.4
  5.9 1.0 %copy-done.4 = f32[16,16,512]{2,1,0:T(8,128)S(1)} copy-done((f32[16,16,512]{2,1,0:T(8,128)S(1)}, f32[16,16,512]{2,1,0:T(8,128)}, u32[]{:S(2)}) %copy-start.4) | copy-done | bytes 524312
  7.0 0.0 copy-start.5
  7.0 1.0 %copy-done.5 = f32[16,16,512]{2,1,0:T(8,128)S(1)} copy-done((f32[16,16,512]{2,1,0:T(8,128)S(1)}, f32[16,16,512]{2,1,0:T(8,128)}, u32[]{:S(2)}) %copy-start.5) | copy-done | bytes 524312
  8.0 0.0 copy-start.6
  8.0 0.7 %copy-done.6 = s32[16]{0:T(128)S(1)} copy-done((s32[16]{0:T(128)S(1)}, s32[16]{0:T(128)}, u32[]{:S(2)}) %copy-start.6) | copy-done | bytes 88
  8.7 35.3 %shard_map.119 = (f32[16,16,512]{2,1,0:T(8,128)S(1)}, f32[2,16,16,512]{3,2,1,0:T(8,128)S(1)}, f32[2,16,16,512]{3,2,1,0:T(8,128)S(1)}, f32[3,16,16,512]{3,2,1,0:T(8,128)S(1)}, f32[16,16,512]{2,1,0:T(8,128)S(1)}) custom-call(s32[16]{0:T(128)S(1)} %copy-done.6, f32[16,4,128]{2,1,0:T(4,128)S(1)} %reshape.16.adjoint_ref, f32[16,4,128]{2,1,0:T(4,128)S(1)} %reshape.17.forward_ref, ...), custom_call_target="tpu_custom_call" | custom-call | tf_op jit(solution)/shard_map/pallas_call | solution.py:396
  44.0 0.8 %copy.22 = f32[16,16,512]{2,1,0:T(8,128)} copy(f32[16,16,512]{2,1,0:T(8,128)S(1)} %get-tuple-element.10) | data formatting | bytes 1048576
  44.8 1.0 %copy.23 = f32[2,16,16,512]{3,2,1,0:T(8,128)} copy(f32[2,16,16,512]{3,2,1,0:T(8,128)S(1)} %get-tuple-element.11) | data formatting | bytes 2097152
  45.7 1.0 %copy.24 = f32[2,16,16,512]{3,2,1,0:T(8,128)} copy(f32[2,16,16,512]{3,2,1,0:T(8,128)S(1)} %get-tuple-element.12) | data formatting | bytes 2097152
  46.7 1.1 %copy.25 = f32[3,16,16,512]{3,2,1,0:T(8,128)} copy(f32[3,16,16,512]{3,2,1,0:T(8,128)S(1)} %get-tuple-element.13) | data formatting | bytes 3145728
  47.9 0.8 %copy.26 = f32[16,16,512]{2,1,0:T(8,128)} copy(f32[16,16,512]{2,1,0:T(8,128)S(1)} %get-tuple-element.14) | data formatting | bytes 1048576
  (2 shorter events, 0.0 us)
Async XLA Ops:
  0.6 1.6 %copy-start.1 = (f32[2,16,16,512]{3,2,1,0:T(8,128)S(1)}, f32[2,16,16,512]{3,2,1,0:T(8,128)}, u32[]{:S(2)}) copy-start(f32[2,16,16,512]{3,2,1,0:T(8,128)} %vector_hbm.1) | copy-start | bytes 3145732
  2.3 1.4 %copy-start = (f32[3,16,16,512]{3,2,1,0:T(8,128)S(1)}, f32[3,16,16,512]{3,2,1,0:T(8,128)}, u32[]{:S(2)}) copy-start(f32[3,16,16,512]{3,2,1,0:T(8,128)} %sym_hbm.1) | copy-start | bytes 4718596
  3.7 1.2 %copy-start.2 = (f32[2,16,16,512]{3,2,1,0:T(8,128)S(1)}, f32[2,16,16,512]{3,2,1,0:T(8,128)}, u32[]{:S(2)}) copy-start(f32[2,16,16,512]{3,2,1,0:T(8,128)} %grad_hbm.1) | copy-start | bytes 3145732
  4.9 1.0 %copy-start.3 = (f32[16,16,512]{2,1,0:T(8,128)S(1)}, f32[16,16,512]{2,1,0:T(8,128)}, u32[]{:S(2)}) copy-start(f32[16,16,512]{2,1,0:T(8,128)} %observed_hbm.1) | copy-start | bytes 1572868
  5.9 1.0 %copy-start.4 = (f32[16,16,512]{2,1,0:T(8,128)S(1)}, f32[16,16,512]{2,1,0:T(8,128)}, u32[]{:S(2)}) copy-start(f32[16,16,512]{2,1,0:T(8,128)} %image_hbm.1) | copy-start | bytes 1572868
  7.0 1.0 %copy-start.5 = (f32[16,16,512]{2,1,0:T(8,128)S(1)}, f32[16,16,512]{2,1,0:T(8,128)}, u32[]{:S(2)}) copy-start(f32[16,16,512]{2,1,0:T(8,128)} %data_hbm.1) | copy-start | bytes 1572868
  8.0 0.7 %copy-start.6 = (s32[16]{0:T(128)S(1)}, s32[16]{0:T(128)}, u32[]{:S(2)}) copy-start(s32[16]{0:T(128)} %index_ref.1) | copy-start | bytes 196

commit v2 on v1

v2 whole, which is shorter than its diff:
```python
import functools

import jax
import jax.numpy as jnp
from jax import lax
from jax.experimental import pallas as pl
from jax.experimental.pallas import tpu as pltpu
from jax.sharding import PartitionSpec as P

FIDELITY = 2.0
STEP_DUAL = 0.25
BOUND_FIRST = 16.0
BOUND_SECOND = 24.0
MESH = pl.DeviceIdType.MESH
F32 = jnp.float32
BF16 = jnp.bfloat16
CHUNK = 4


def split(value):
    high = value.astype(BF16)
    return high, (value - high.astype(F32)).astype(BF16)


def build_tables(kernels_ref, table_ref):
    size, count, _ = kernels_ref.shape
    groups = []
    for half in range(2):
        total = jnp.zeros((count, 128), F32)
        for i in range(8 * half, min(size, 8 * half + 8)):
            slab = jnp.concatenate([kernels_ref[i], jnp.zeros((count, 128 - size), F32)], 1)
            total = total + (pltpu.roll(slab, 16 * (i % 8), 1) if i % 8 else slab)
        groups.append(total)
    high, low = split(jnp.concatenate(groups, 1))
    values = jnp.concatenate([high, low], 0)
    line = lax.broadcasted_iota(jnp.int32, (256, 128), 0)
    lane = lax.broadcasted_iota(jnp.int32, (256, 128), 1)
    b, i = lane // 32, lane % 32
    for t, factor in enumerate((-0.5, STEP_DUAL)):
        for a in range(4):
            j = 4 * a + b
            place = 16 * (size - 1 - i) + size - 1 - j if t == 0 else 16 * i + j
            place = jnp.where((i < size) & (j < size), place, -1)
            chosen = jnp.where(line == place, 1.0, 0.0).astype(BF16)
            both = jnp.dot(values, chosen, preferred_element_type=F32)
            table_ref[t, a] = factor * (both[:count] + both[count:])


def table_row(table_ref, t, a, index):
    return jnp.broadcast_to(table_ref[t, a, pl.ds(index, 1), :], (8, 128))


def toeplitz_scatter(table_ref, index):
    lane = lax.broadcasted_iota(jnp.int32, (8, 128), 1)
    first = lane % 32 < 16
    groups = []
    for a in range(4):
        row = table_row(table_ref, 0, a, index)
        for base in (0, 8, -8, 16):
            moved = pltpu.roll(row, (base - 7) % 128, 1, stride=1, stride_axis=0)
            groups.append(jnp.where(first, moved, pltpu.roll(moved, 16, 1)))
    return jnp.concatenate(split(jnp.concatenate(groups, 0)), 1)


def toeplitz_gather(table_ref, index):
    lane = lax.broadcasted_iota(jnp.int32, (8, 128), 1) % 32
    groups = []
    for a in range(4):
        row = table_row(table_ref, 1, a, index)
        for base in (0, 8):
            own = pltpu.roll(row, (base - 7) % 128, 1, stride=1, stride_axis=0)
            above = pltpu.roll(row, base + 17, 1, stride=1, stride_axis=0)
            below = pltpu.roll(row, base + 1, 1, stride=1, stride_axis=0)
            groups.append(jnp.where(lane < 16, own, jnp.where(lane < 24, above, below)))
    high, low = split(jnp.concatenate(groups, 0))
    return jnp.concatenate([high, high, low], 1)


def padded_shifts(field):
    rows, cols = field.shape
    wide = jnp.concatenate([field, jnp.zeros((rows, 128), F32)], 1)
    return [split(wide if b == 3 else pltpu.roll(wide, 3 - b, 1)) for b in range(4)]


def gather_shifts(product, rows, cols):
    width = product.shape[1]
    total = product[rows : 2 * rows]
    for a in (0, 2, 3):
        total = total + pltpu.roll(product[a * rows : (a + 1) * rows], (4 - 4 * a) % width, 1)
    return total[:, :cols]


def column_before(field):
    lane = lax.broadcasted_iota(jnp.int32, field.shape, 1)
    return jnp.where(lane == 0, 0.0, pltpu.roll(field, 1, 1))


def column_after(field):
    cols = field.shape[1]
    lane = lax.broadcasted_iota(jnp.int32, field.shape, 1)
    return jnp.where(lane == cols - 1, 0.0, pltpu.roll(field, cols - 1, 1))


def row_before(field, first):
    line = lax.broadcasted_iota(jnp.int32, field.shape, 0)
    return jnp.where(line == 0, first, pltpu.roll(field, 1, 0))


def row_after(field, last):
    rows = field.shape[0]
    line = lax.broadcasted_iota(jnp.int32, field.shape, 0)
    return jnp.where(line == rows - 1, last, pltpu.roll(field, rows - 1, 0))


def kernel(
    bands, rows, cols, band_axis, row_axis,
    index_hbm, kernels_hbm, observed_hbm, image_hbm, vector_hbm, grad_hbm, sym_hbm, data_hbm,
    img, vec, grad, sym, data, scales,
    index_ref, kernels_ref, table, obs, bar, gather_w,
    line_up, line_dn, line_from_dn, line_from_up,
    near_up, near_dn, near_from_dn, near_from_up,
    far_up, far_dn, far_from_dn, far_from_up,
    norms, mate_in, chip_sum, chip_in,
    in_sem, data_sem, line_send, line_recv, near_send, near_recv, far_send, far_recv,
    mate_send, mate_recv, chip_send, chip_recv, back_send, back_recv,
):
    me_row, me_band = lax.axis_index("row"), lax.axis_index("band")
    core, chip = lax.rem(me_band, 2), me_band // 2
    mate = me_band + 1 - 2 * core
    chip_count = band_axis // 2
    peers = [lax.rem(me_band + 2 * k, band_axis) for k in range(1, chip_count)]
    has_up, has_down = me_row > 0, me_row < row_axis - 1
    up, down = me_row - 1, me_row + 1
    not_top = jnp.where(has_up, 1.0, 0.0).astype(F32)
    not_end = jnp.where(has_down, 1.0, 0.0).astype(F32)
    chunks = bands // CHUNK

    barrier = pltpu.get_barrier_semaphore()

    def greet(**target):
        pl.semaphore_signal(barrier, inc=1, device_id=target, device_id_type=MESH)

    pl.when(has_up)(lambda: greet(row=up))
    pl.when(has_down)(lambda: greet(row=down))
    greet(band=mate)
    for peer in peers:
        greet(band=peer)

    def fetch(source, target, sem):
        copy = pltpu.make_async_copy(source, target, sem)
        copy.start()
        return copy

    load_index = fetch(index_hbm, index_ref, in_sem.at[0])
    load_kernels = fetch(kernels_hbm, kernels_ref, in_sem.at[1])
    load_sym = fetch(sym_hbm, sym, in_sem.at[2])
    load_grad = fetch(grad_hbm, grad, in_sem.at[3])
    load_vec = fetch(vector_hbm, vec, in_sem.at[4])
    load_data = fetch(data_hbm, data, in_sem.at[5])
    load_img = fetch(image_hbm, img, in_sem.at[6])
    load_obs = fetch(observed_hbm, obs, in_sem.at[7])

    def remote(source, target, send, recv, **which):
        return pltpu.make_async_remote_copy(
            src_ref=source, dst_ref=target, send_sem=send, recv_sem=recv,
            device_id=which, device_id_type=MESH,
        )

    def line_copies():
        return (
            remote(line_up, line_from_dn, line_send.at[0], line_recv.at[0], row=up),
            remote(line_dn, line_from_up, line_send.at[1], line_recv.at[1], row=down),
        )

    def near_copies(c):
        return (
            remote(near_up.at[c], near_from_dn.at[c], near_send.at[0, c], near_recv.at[0, c], row=up),
            remote(near_dn.at[c], near_from_up.at[c], near_send.at[1, c], near_recv.at[1, c], row=down),
        )

    def far_copies(c):
        body = pl.ds(8, 6 * CHUNK)
        return (
            remote(far_up.at[c, body], far_from_dn.at[c, body], far_send.at[0, c], far_recv.at[0, c], row=up),
            remote(far_dn.at[c, body], far_from_up.at[c, body], far_send.at[1, c], far_recv.at[1, c], row=down),
        )

    def start(copies):
        pl.when(has_up)(copies[0].start)
        pl.when(has_down)(copies[1].start)

    def wait_recv(copies):
        pl.when(has_down)(copies[0].wait_recv)
        pl.when(has_up)(copies[1].wait_recv)

    def wait_send(copies):
        pl.when(has_up)(copies[0].wait_send)
        pl.when(has_down)(copies[1].wait_send)

    @pl.when(jnp.logical_not(has_up))
    def _():
        for ref in (line_from_up, near_from_up, far_from_up):
            ref[...] = jnp.zeros(ref.shape, F32)

    @pl.when(jnp.logical_not(has_down))
    def _():
        for ref in (line_from_dn, near_from_dn, far_from_dn):
            ref[...] = jnp.zeros(ref.shape, F32)

    load_kernels.wait()
    build_tables(kernels_ref, table)

    load_sym.wait()
    load_grad.wait()
    load_vec.wait()

    def pack_lines(c, carry):
        for k in range(CHUNK):
            band = c * CHUNK + k
            top = pl.ds(0, 1)
            cross, p0, p1 = sym[2, band, top, :], grad[0, band, top, :], grad[1, band, top, :]
            q0, q1 = sym[0, band, top, :], sym[1, band, top, :]
            line_up[0, band] = vec[0, band, top, :] + 0.5 * (q0 - (column_before(cross) - cross) + p0)
            line_up[1, band] = vec[1, band, top, :] + 0.5 * (cross - (column_before(q1) - q1) + p1)
            line_dn[0, band] = sym[0, band, pl.ds(rows - 1, 1), :]
            line_dn[1, band] = sym[2, band, pl.ds(rows - 1, 1), :]
        return carry

    lax.fori_loop(0, chunks, pack_lines, 0)
    pl.semaphore_wait(barrier, 1 + len(peers) + has_up.astype(jnp.int32) + has_down.astype(jnp.int32))
    start(line_copies())

    load_index.wait()
    load_data.wait()
    load_img.wait()
    tile_line = lax.broadcasted_iota(jnp.int32, (8, cols), 0)

    def adjoint(c, carry):
        for k in range(CHUNK):
            band = c * CHUNK + k
            parts = [part for pair in padded_shifts(data[band]) for part in pair]
            stacked = jnp.concatenate(parts + parts, 0)
            weights = toeplitz_scatter(table, index_ref[band])
            product = jnp.dot(weights, stacked, preferred_element_type=F32)
            total = gather_shifts(product, 2 * rows, cols)
            p0, p1 = grad[0, band], grad[1, band]
            own = img[band] + total[:rows] - 0.5 * (row_before(p0, 0.0) - p0 + column_before(p1) - p1)
            bar[band] = own
            above, below = total[rows : rows + 8], total[rows + 8 : rows + 16]
            near_up[c, k] = jnp.where(tile_line == 0, own[:8], above)
            below = below - jnp.where(tile_line == 0, 0.5 * pltpu.roll(p0[8:], 1, 0), 0.0)
            near_dn[c, k] = jnp.where(tile_line == 7, own[8:], below)
            far_up[c, pl.ds(8 + 6 * k, 6), :] = own[1:7]
            far_dn[c, pl.ds(8 + 6 * k, 6), :] = own[9:15]
        start(near_copies(c))
        return carry

    lax.fori_loop(0, chunks, adjoint, 0)

    def start_far(c, carry):
        start(far_copies(c))
        return carry

    lax.fori_loop(0, chunks, start_far, 0)

    wait_recv(line_copies())

    def symmetric(step, norm):
        for k in range(2):
            band = 2 * step + k
            q0, q1, q2 = sym[0, band], sym[1, band], sym[2, band]
            p0, p1 = grad[0, band], grad[1, band]
            v0, v1 = vec[0, band], vec[1, band]
            prev0, prev2 = not_top * line_from_up[0, band], not_top * line_from_up[1, band]
            step0 = 0.25 * (row_before(q0, prev0) - q0 + column_before(q2) - q2 - p0)
            step1 = 0.25 * (column_before(q1) - q1 + row_before(q2, prev2) - q2 - p1)
            vec[0, band] = v0 - step0
            vec[1, band] = v1 - step1
            bar0, bar1 = v0 - 2.0 * step0, v1 - 2.0 * step1
            end = pl.ds(rows - 1, 1)
            next0 = not_end * (line_from_dn[0, band] - 0.5 * sym[0, band, end, :])
            next1 = not_end * (line_from_dn[1, band] - 0.5 * sym[2, band, end, :])
            new0 = q0 + 0.25 * (row_after(bar0, next0) - bar0)
            new1 = q1 + 0.25 * (column_after(bar1) - bar1)
            new2 = q2 + 0.125 * (column_after(bar0) - bar0 + row_after(bar1, next1) - bar1)
            sym[0, band] = new0
            sym[1, band] = new1
            sym[2, band] = new2
            grad[0, band] = p0 - 0.25 * bar0
            grad[1, band] = p1 - 0.25 * bar1
            norm = norm + (new0 * new0 + new1 * new1 + 2.0 * (new2 * new2))
        return norm

    def mate_copy(which):
        return remote(norms.at[which, 1 - core], mate_in.at[which], mate_send.at[which], mate_recv.at[which], band=mate)

    def chip_copy(which, peer, slot):
        return remote(
            chip_sum.at[which], chip_in.at[which, slot],
            chip_send.at[which, peer // 2], chip_recv.at[which, slot], band=peer,
        )

    def back_copy(which, half):
        return remote(scales.at[which, core], scales.at[which, half], back_send.at[which], back_recv.at[which], band=mate)

    def send_norm(which, norm):
        norms[which, 0] = norm[:8]
        norms[which, 1] = norm[8:]
        mate_copy(which).start()

    def send_chip(which):
        mate_copy(which).wait()
        total = norms[which, core] + mate_in[which]
        chip_sum[which] = total
        chip_in[which, chip] = total
        for peer in peers:
            chip_copy(which, peer, chip).start()

    def send_scale(which, bound):
        for peer in peers:
            chip_copy(which, peer, peer // 2).wait()
        total = chip_in[which, 0]
        for other in range(1, chip_count):
            total = total + chip_in[which, other]
        scales[which, core] = 1.0 / jnp.maximum(1.0, jnp.sqrt(total) * (1.0 / bound))
        back_copy(which, core).start()

    norm_sym = lax.fori_loop(0, bands // 2, symmetric, jnp.zeros((rows, cols), F32))
    send_norm(0, norm_sym)

    def gather_weights(band, carry):
        gather_w[band] = toeplitz_gather(table, index_ref[band])
        return carry

    lax.fori_loop(0, bands, gather_weights, 0)
    send_chip(0)

    def first_order(c, norm):
        wait_recv(near_copies(c))
        for k in range(CHUNK):
            band = c * CHUNK + k
            part = bar[band]
            from_up, from_dn = near_from_up[c, k], near_from_dn[c, k]
            top = part[:8] + jnp.where(tile_line == 7, 0.0, not_top * from_up)
            end = part[8:] + jnp.where(tile_line == 0, 0.0, not_end * from_dn)
            own = jnp.concatenate([top, end], 0)
            bar[band] = own
            img[band] = 0.5 * (img[band] + own)
            following = not_end * (near_from_dn[c, k, pl.ds(0, 1), :] + near_dn[c, k, pl.ds(0, 1), :])
            new0 = grad[0, band] + 0.25 * (row_after(own, following) - own)
            new1 = grad[1, band] + 0.25 * (column_after(own) - own)
            grad[0, band] = new0
            grad[1, band] = new1
            norm = norm + (new0 * new0 + new1 * new1)
        return norm

    norm_grad = lax.fori_loop(0, chunks, first_order, jnp.zeros((rows, cols), F32))
    send_norm(1, norm_grad)
    load_obs.wait()
    send_chip(1)

    def forward(c, carry):
        wait_recv(far_copies(c))
        for k in range(CHUNK):
            band = c * CHUNK + k
            middle = (tile_line >= 1) & (tile_line <= 6)
            near = pl.ds(7 + 6 * k, 8)
            above = jnp.where(middle, far_from_up[c, near, :], near_from_up[c, k])
            above = not_top * jnp.where(tile_line == 0, 0.0, above + near_up[c, k])
            below = jnp.where(middle, far_from_dn[c, near, :], near_from_dn[c, k])
            below = not_end * jnp.where(tile_line == 7, 0.0, below + near_dn[c, k])
            pairs = padded_shifts(jnp.concatenate([bar[band], above, below], 0))
            highs, lows = [pair[0] for pair in pairs], [pair[1] for pair in pairs]
            stacked = jnp.concatenate(highs + lows + highs, 0)
            product = jnp.dot(gather_w[band], stacked, preferred_element_type=F32)
            blurred = gather_shifts(product, rows, cols)
            data[band] = (data[band] + (blurred - STEP_DUAL * obs[band])) * (1.0 / (1.0 + STEP_DUAL / FIDELITY))
        return carry

    lax.fori_loop(0, chunks, forward, 0)
    send_scale(0, BOUND_SECOND)
    send_scale(1, BOUND_FIRST)

    wait_send(line_copies())

    def finish(c, carry):
        wait_send(near_copies(c))
        wait_send(far_copies(c))
        return carry

    lax.fori_loop(0, chunks, finish, 0)
    for which in range(2):
        back_copy(which, 1 - core).wait()


def finish_kernel(
    img, vec, grad, sym, data, scales,
    image_out, vector_out, grad_out, sym_out, data_out,
    scaled_sym, scaled_grad, plain_sem, sym_sem, grad_sem,
):
    plain = [
        pltpu.make_async_copy(source, target, plain_sem.at[k])
        for k, (source, target) in enumerate(((vec, vector_out), (img, image_out), (data, data_out)))
    ]
    for copy in plain:
        copy.start()
    chunks = img.shape[0] // CHUNK
    factor_sym = jnp.concatenate([scales[0, 0], scales[0, 1]], 0)
    factor_grad = jnp.concatenate([scales[1, 0], scales[1, 1]], 0)

    def stores(c):
        part = pl.ds(c * CHUNK, CHUNK)
        return (
            pltpu.make_async_copy(scaled_sym.at[:, part], sym_out.at[:, part], sym_sem.at[c]),
            pltpu.make_async_copy(scaled_grad.at[:, part], grad_out.at[:, part], grad_sem.at[c]),
        )

    def scale(c, carry):
        for k in range(CHUNK):
            band = c * CHUNK + k
            for part in range(3):
                scaled_sym[part, band] = sym[part, band] * factor_sym
            for part in range(2):
                scaled_grad[part, band] = grad[part, band] * factor_grad
        for copy in stores(c):
            copy.start()
        return carry

    lax.fori_loop(0, chunks, scale, 0)

    def wait(c, carry):
        for copy in stores(c):
            copy.wait()
        return carry

    lax.fori_loop(0, chunks, wait, 0)
    for copy in plain:
        copy.wait()


def body(band_axis, row_axis, observed, image, vector_field, dual_grad, dual_sym, dual_data, kernels, kernel_index):
    bands, rows, cols = image.shape
    chunks = bands // CHUNK
    turned = jnp.transpose(kernels, (1, 0, 2))
    size, count, _ = turned.shape
    vmem, hbm, dma = pltpu.VMEM, pltpu.HBM, pltpu.SemaphoreType.DMA
    near, far = (chunks, CHUNK, 8, cols), (chunks, 16 + 6 * CHUNK, cols)
    line, half = (2, bands, 1, cols), (8, cols)
    anywhere = pl.BlockSpec(memory_space=pl.ANY)
    inside = pl.BlockSpec(memory_space=pltpu.VMEM)
    results = (image, vector_field, dual_grad, dual_sym, dual_data)
    inputs = (kernel_index, turned, observed, image, vector_field, dual_grad, dual_sym, dual_data)
    held = pl.pallas_call(
        functools.partial(kernel, bands, rows, cols, band_axis, row_axis),
        out_shape=[vmem(a.shape, F32) for a in results] + [vmem((2, 2, *half), F32)],
        in_specs=[anywhere] * 8,
        out_specs=[inside] * 6,
        scratch_shapes=[
            pltpu.SMEM(kernel_index.shape, jnp.int32),
            vmem((size, count, size), F32),
            vmem((2, 4, count, 128), F32),
            vmem(image.shape, F32),
            vmem(image.shape, F32),
            vmem((bands, 4 * rows, 384), BF16),
        ]
        + [vmem(line, F32)] * 4
        + [vmem(near, F32)] * 4
        + [vmem(far, F32)] * 4
        + [vmem((2, 2, *half), F32), vmem((2, *half), F32), vmem((2, *half), F32), vmem((2, band_axis // 2, *half), F32)]
        + [dma((8,)), dma((1,)), dma((2,)), dma((2,))]
        + [dma((2, chunks))] * 4
        + [dma((2,))] * 2
        + [dma((2, band_axis // 2))] * 2
        + [dma((2,))] * 2,
        compiler_params=pltpu.CompilerParams(
            collective_id=0, has_side_effects=True, vmem_limit_bytes=24 * 1024 * 1024
        ),
    )(*[pltpu.with_memory_space_constraint(a, hbm) for a in inputs])
    return pl.pallas_call(
        finish_kernel,
        out_shape=[hbm(a.shape, F32) for a in results],
        in_specs=[inside] * 6,
        out_specs=[anywhere] * 5,
        scratch_shapes=[vmem(dual_sym.shape, F32), vmem(dual_grad.shape, F32), dma((3,)), dma((chunks,)), dma((chunks,))],
        compiler_params=pltpu.CompilerParams(vmem_limit_bytes=16 * 1024 * 1024),
    )(*[pltpu.with_memory_space_constraint(a, vmem) for a in held])


def solution(mesh):
    placed = (
        P("band", "row", None),
        P("band", "row", None),
        P(None, "band", "row", None),
        P(None, "band", "row", None),
        P(None, "band", "row", None),
        P("band", "row", None),
        P(),
        P("band"),
    )
    return jax.shard_map(
        functools.partial(body, mesh.shape["band"], mesh.shape["row"]),
        mesh=mesh,
        in_specs=placed,
        out_specs=(
            P("band", "row", None),
            P(None, "band", "row", None),
            P(None, "band", "row", None),
            P(None, "band", "row", None),
            P("band", "row", None),
        ),
        check_vma=False,
    )
```

time: 49 us -> 29.7 us (0.61)
  the two profiles are of different devices: /device:TPU:1 before, /device:TPU:25 now
where the time goes in v2:
time: 29.7 us
  Pallas kernels  29 us (98%)
  between operations  0.64 us (2%)
    pallas_call x1, Pallas kernels, body(): pl.pallas_call(functools.partial(kernel, bands, rows, cols, band_axis, ro...  26.8 us
    pallas_call x1, Pallas kernels, body(): pl.pallas_call(finish_kernel, out_shape=[hbm(a.shape, F32) for a in resul...  2.27 us

profile of v2, /device:TPU:25, one launch (start us, length us, event | category | flops | bytes accessed | tf_op | source)
XLA Modules:
  0.0 29.7 jit_solution(11360400829145298018)
XLA Ops:
  0.6 26.8 %shard_map.119 = (f32[16,16,512]{2,1,0:T(8,128)S(1)}, f32[2,16,16,512]{3,2,1,0:T(8,128)S(1)}, f32[2,16,16,512]{3,2,1,0:T(8,128)S(1)}, f32[3,16,16,512]{3,2,1,0:T...) custom-call(s32[16]{0:T(128)} %index_hbm.1, f32[15,16,15]{2,1,0:T(8,128)} %bitcast.1, ...), custom_call_target="tpu_custom_call" | custom-call | tf_op jit(solution)/shard_map/pallas_call | solution.py:453
  27.4 2.3 %shard_map.120 = (f32[16,16,512]{2,1,0:T(8,128)}, f32[2,16,16,512]{3,2,1,0:T(8,128)}, f32[2,16,16,512]{3,2,1,0:T(8,128)}, f32[3,16,16,512]{3,2,1,0:T(8,128)}, f32[16,16,512]{2,1,0:T(8,128)}) custom-call(f32[16,16,512]{2,1,0:T(8,128)S(1)} %get-tuple-element.11.img, f32[2,16,16,512]{3,2,1,0:T(8,128)S(1)} %get-tuple-element.12.vec, ...), custom_call_target="tpu_custom_call" | custom-call | tf_op jit(solution)/shard_map/pallas_call | solution.py:479

commit v3 on v2

--- a/solution.py
+++ b/solution.py
@@ -122,7 +122,7 @@
     far_up, far_dn, far_from_dn, far_from_up,
     norms, mate_in, chip_sum, chip_in,
     in_sem, data_sem, line_send, line_recv, near_send, near_recv, far_send, far_recv,
-    mate_send, mate_recv, chip_send, chip_recv, back_send, back_recv,
+    mate_send, mate_recv, chip_send, chip_recv, back_send, back_recv, ready,
 ):
     me_row, me_band = lax.axis_index("row"), lax.axis_index("band")
     core, chip = lax.rem(me_band, 2), me_band // 2
@@ -144,7 +144,7 @@
     pl.when(has_down)(lambda: greet(row=down))
     greet(band=mate)
     for peer in peers:
-        greet(band=peer)
+        pl.when(peer > me_band)(functools.partial(greet, band=peer))
 
     def fetch(source, target, sem):
         copy = pltpu.make_async_copy(source, target, sem)
@@ -214,20 +214,21 @@
     load_grad.wait()
     load_vec.wait()
 
-    def pack_lines(c, carry):
-        for k in range(CHUNK):
-            band = c * CHUNK + k
-            top = pl.ds(0, 1)
-            cross, p0, p1 = sym[2, band, top, :], grad[0, band, top, :], grad[1, band, top, :]
-            q0, q1 = sym[0, band, top, :], sym[1, band, top, :]
-            line_up[0, band] = vec[0, band, top, :] + 0.5 * (q0 - (column_before(cross) - cross) + p0)
-            line_up[1, band] = vec[1, band, top, :] + 0.5 * (cross - (column_before(q1) - q1) + p1)
-            line_dn[0, band] = sym[0, band, pl.ds(rows - 1, 1), :]
-            line_dn[1, band] = sym[2, band, pl.ds(rows - 1, 1), :]
-        return carry
-
-    lax.fori_loop(0, chunks, pack_lines, 0)
-    pl.semaphore_wait(barrier, 1 + len(peers) + has_up.astype(jnp.int32) + has_down.astype(jnp.int32))
+    def lines_of(ref, part, row):
+        return ref[part, :, row, :]
+
+    q0, q1, cross = [lines_of(sym, part, 0) for part in range(3)]
+    line_up[0] = lines_of(vec, 0, 0) + 0.5 * (q0 - (column_before(cross) - cross) + lines_of(grad, 0, 0))
+    line_up[1] = lines_of(vec, 1, 0) + 0.5 * (cross - (column_before(q1) - q1) + lines_of(grad, 1, 0))
+    line_dn[0] = lines_of(sym, 0, rows - 1)
+    line_dn[1] = lines_of(sym, 2, rows - 1)
+    pl.semaphore_wait(barrier, 1 + chip + has_up.astype(jnp.int32) + has_down.astype(jnp.int32))
+
+    def answer(peer):
+        pl.semaphore_signal(ready, inc=1, device_id={"band": peer}, device_id_type=MESH)
+
+    for peer in peers:
+        pl.when(peer < me_band)(functools.partial(answer, peer))
     start(line_copies())
 
     load_index.wait()
@@ -259,9 +260,9 @@
 
     def start_far(c, carry):
         start(far_copies(c))
-        return carry
-
-    lax.fori_loop(0, chunks, start_far, 0)
+
+
+    pl.when(chip < chip_count // 2)(lambda: lax.fori_loop(0, chunks, start_far, None))
 
     wait_recv(line_copies())
 
@@ -271,15 +272,16 @@
             q0, q1, q2 = sym[0, band], sym[1, band], sym[2, band]
             p0, p1 = grad[0, band], grad[1, band]
             v0, v1 = vec[0, band], vec[1, band]
-            prev0, prev2 = not_top * line_from_up[0, band], not_top * line_from_up[1, band]
+            here = pl.ds(band, 1)
+            prev0, prev2 = not_top * line_from_up[0, here, :], not_top * line_from_up[1, here, :]
             step0 = 0.25 * (row_before(q0, prev0) - q0 + column_before(q2) - q2 - p0)
             step1 = 0.25 * (column_before(q1) - q1 + row_before(q2, prev2) - q2 - p1)
             vec[0, band] = v0 - step0
             vec[1, band] = v1 - step1
             bar0, bar1 = v0 - 2.0 * step0, v1 - 2.0 * step1
             end = pl.ds(rows - 1, 1)
-            next0 = not_end * (line_from_dn[0, band] - 0.5 * sym[0, band, end, :])
-            next1 = not_end * (line_from_dn[1, band] - 0.5 * sym[2, band, end, :])
+            next0 = not_end * (line_from_dn[0, here, :] - 0.5 * sym[0, band, end, :])
+            next1 = not_end * (line_from_dn[1, here, :] - 0.5 * sym[2, band, end, :])
             new0 = q0 + 0.25 * (row_after(bar0, next0) - bar0)
             new1 = q1 + 0.25 * (column_after(bar1) - bar1)
             new2 = q2 + 0.125 * (column_after(bar0) - bar0 + row_after(bar1, next1) - bar1)
@@ -333,6 +335,7 @@
         return carry
 
     lax.fori_loop(0, bands, gather_weights, 0)
+    pl.when(chip < chip_count - 1)(lambda: pl.semaphore_wait(ready, chip_count - 1 - chip))
     send_chip(0)
 
     def first_order(c, norm):
@@ -356,8 +359,10 @@
 
     norm_grad = lax.fori_loop(0, chunks, first_order, jnp.zeros((rows, cols), F32))
     send_norm(1, norm_grad)
+    pl.when(chip >= chip_count // 2)(lambda: lax.fori_loop(0, 1, start_far, None))
     load_obs.wait()
     send_chip(1)
+    pl.when(chip >= chip_count // 2)(lambda: lax.fori_loop(1, chunks, start_far, None))
 
     def forward(c, carry):
         wait_recv(far_copies(c))
@@ -445,7 +450,7 @@
     size, count, _ = turned.shape
     vmem, hbm, dma = pltpu.VMEM, pltpu.HBM, pltpu.SemaphoreType.DMA
     near, far = (chunks, CHUNK, 8, cols), (chunks, 16 + 6 * CHUNK, cols)
-    line, half = (2, bands, 1, cols), (8, cols)
+    line, half = (2, bands, cols), (8, cols)
     anywhere = pl.BlockSpec(memory_space=pl.ANY)
     inside = pl.BlockSpec(memory_space=pltpu.VMEM)
     results = (image, vector_field, dual_grad, dual_sym, dual_data)
@@ -471,7 +476,8 @@
         + [dma((2, chunks))] * 4
         + [dma((2,))] * 2
         + [dma((2, band_axis // 2))] * 2
-        + [dma((2,))] * 2,
+        + [dma((2,))] * 2
+        + [pltpu.SemaphoreType.REGULAR],
         compiler_params=pltpu.CompilerParams(
             collective_id=0, has_side_effects=True, vmem_limit_bytes=24 * 1024 * 1024
         ),

time: 29.7 us -> 29.6 us (level)
  no operation moved by 1% of the time
where the time goes in v3:
time: 29.6 us; the launch traced here: 29.5 us
  Pallas kernels  28.9 us (98%)
  between operations  0.64 us (2%)
    pallas_call x1, Pallas kernels, body(): pl.pallas_call(functools.partial(kernel, bands, rows, cols, band_axis, ro...  26.6 us
    pallas_call x1, Pallas kernels, body(): pl.pallas_call(finish_kernel, out_shape=[hbm(a.shape, F32) for a in resul...  2.27 us

profile of v3, /device:TPU:25, one launch (start us, length us, event | category | flops | bytes accessed | tf_op | source)
XLA Modules:
  0.0 29.5 jit_solution(18176238812219876414)
XLA Ops:
  0.6 26.6 %shard_map.119 = (f32[16,16,512]{2,1,0:T(8,128)S(1)}, f32[2,16,16,512]{3,2,1,0:T(8,128)S(1)}, f32[2,16,16,512]{3,2,1,0:T(8,128)S(1)}, f32[3,16,16,512]{3,2,1,0:T...) custom-call(s32[16]{0:T(128)} %index_hbm.1, f32[15,16,15]{2,1,0:T(8,128)} %bitcast.1, ...), custom_call_target="tpu_custom_call" | custom-call | tf_op jit(solution)/shard_map/pallas_call | solution.py:458
  27.3 2.3 %shard_map.120 = (f32[16,16,512]{2,1,0:T(8,128)}, f32[2,16,16,512]{3,2,1,0:T(8,128)}, f32[2,16,16,512]{3,2,1,0:T(8,128)}, f32[3,16,16,512]{3,2,1,0:T(8,128)}, f32[16,16,512]{2,1,0:T(8,128)}) custom-call(f32[16,16,512]{2,1,0:T(8,128)S(1)} %get-tuple-element.11.img, f32[2,16,16,512]{3,2,1,0:T(8,128)S(1)} %get-tuple-element.12.vec, ...), custom_call_target="tpu_custom_call" | custom-call | tf_op jit(solution)/shard_map/pallas_call | solution.py:485

commit v4 on v3

--- a/solution.py
+++ b/solution.py
@@ -153,12 +153,16 @@
 
     load_index = fetch(index_hbm, index_ref, in_sem.at[0])
     load_kernels = fetch(kernels_hbm, kernels_ref, in_sem.at[1])
-    load_sym = fetch(sym_hbm, sym, in_sem.at[2])
-    load_grad = fetch(grad_hbm, grad, in_sem.at[3])
-    load_vec = fetch(vector_hbm, vec, in_sem.at[4])
-    load_data = fetch(data_hbm, data, in_sem.at[5])
-    load_img = fetch(image_hbm, img, in_sem.at[6])
-    load_obs = fetch(observed_hbm, obs, in_sem.at[7])
+    def fetch_rows(source, target, first, sem):
+        part = (slice(None), slice(None), pl.ds(first, 8))
+        return fetch(source.at[part], target.at[part], sem)
+
+    fields = ((sym_hbm, sym), (grad_hbm, grad), (vector_hbm, vec))
+    load_upper = [fetch_rows(*pair, 0, in_sem.at[2 + k]) for k, pair in enumerate(fields)]
+    load_lower = [fetch_rows(*pair, 8, in_sem.at[5 + k]) for k, pair in enumerate(fields)]
+    load_data = fetch(data_hbm, data, in_sem.at[8])
+    load_img = fetch(image_hbm, img, in_sem.at[9])
+    load_obs = fetch(observed_hbm, obs, in_sem.at[10])
 
     def remote(source, target, send, recv, **which):
         return pltpu.make_async_remote_copy(
@@ -210,9 +214,8 @@
     load_kernels.wait()
     build_tables(kernels_ref, table)
 
-    load_sym.wait()
-    load_grad.wait()
-    load_vec.wait()
+    for load in load_upper:
+        load.wait()
 
     def lines_of(ref, part, row):
         return ref[part, :, row, :]
@@ -220,16 +223,19 @@
     q0, q1, cross = [lines_of(sym, part, 0) for part in range(3)]
     line_up[0] = lines_of(vec, 0, 0) + 0.5 * (q0 - (column_before(cross) - cross) + lines_of(grad, 0, 0))
     line_up[1] = lines_of(vec, 1, 0) + 0.5 * (cross - (column_before(q1) - q1) + lines_of(grad, 1, 0))
+    pl.semaphore_wait(barrier, 1 + chip + has_up.astype(jnp.int32) + has_down.astype(jnp.int32))
+
+    def answer(peer):
+        pl.semaphore_signal(ready, inc=1, device_id={"band": peer}, device_id_type=MESH)
+
+    for peer in peers:
+        pl.when(peer < me_band)(functools.partial(answer, peer))
+    pl.when(has_up)(line_copies()[0].start)
+    for load in load_lower:
+        load.wait()
     line_dn[0] = lines_of(sym, 0, rows - 1)
     line_dn[1] = lines_of(sym, 2, rows - 1)
-    pl.semaphore_wait(barrier, 1 + chip + has_up.astype(jnp.int32) + has_down.astype(jnp.int32))
-
-    def answer(peer):
-        pl.semaphore_signal(ready, inc=1, device_id={"band": peer}, device_id_type=MESH)
-
-    for peer in peers:
-        pl.when(peer < me_band)(functools.partial(answer, peer))
-    start(line_copies())
+    pl.when(has_down)(line_copies()[1].start)
 
     load_index.wait()
     load_data.wait()
@@ -472,7 +478,7 @@
         + [vmem(near, F32)] * 4
         + [vmem(far, F32)] * 4
         + [vmem((2, 2, *half), F32), vmem((2, *half), F32), vmem((2, *half), F32), vmem((2, band_axis // 2, *half), F32)]
-        + [dma((8,)), dma((1,)), dma((2,)), dma((2,))]
+        + [dma((11,)), dma((1,)), dma((2,)), dma((2,))]
         + [dma((2, chunks))] * 4
         + [dma((2,))] * 2
         + [dma((2, band_axis // 2))] * 2

time: 29.6 us -> 29.3 us (0.990)
  Pallas kernels: 28.9 us -> 28.6 us
where the time goes in v4:
time: 29.3 us
  Pallas kernels  28.6 us (98%)
  between operations  0.64 us (2%)
    pallas_call x1, Pallas kernels, body(): pl.pallas_call(functools.partial(kernel, bands, rows, cols, band_axis, ro...  26.4 us
    pallas_call x1, Pallas kernels, body(): pl.pallas_call(finish_kernel, out_shape=[hbm(a.shape, F32) for a in resul...  2.27 us

profile of v4, /device:TPU:25, one launch (start us, length us, event | category | flops | bytes accessed | tf_op | source)
XLA Modules:
  0.0 29.3 jit_solution(6793418925110984182)
XLA Ops:
  0.6 26.4 %shard_map.119 = (f32[16,16,512]{2,1,0:T(8,128)S(1)}, f32[2,16,16,512]{3,2,1,0:T(8,128)S(1)}, f32[2,16,16,512]{3,2,1,0:T(8,128)S(1)}, f32[3,16,16,512]{3,2,1,0:T...) custom-call(s32[16]{0:T(128)} %index_hbm.1, f32[15,16,15]{2,1,0:T(8,128)} %bitcast.1, ...), custom_call_target="tpu_custom_call" | custom-call | tf_op jit(solution)/shard_map/pallas_call | solution.py:464
  27.0 2.3 %shard_map.120 = (f32[16,16,512]{2,1,0:T(8,128)}, f32[2,16,16,512]{3,2,1,0:T(8,128)}, f32[2,16,16,512]{3,2,1,0:T(8,128)}, f32[3,16,16,512]{3,2,1,0:T(8,128)}, f32[16,16,512]{2,1,0:T(8,128)}) custom-call(f32[16,16,512]{2,1,0:T(8,128)S(1)} %get-tuple-element.11.img, f32[2,16,16,512]{3,2,1,0:T(8,128)S(1)} %get-tuple-element.12.vec, ...), custom_call_target="tpu_custom_call" | custom-call | tf_op jit(solution)/shard_map/pallas_call | solution.py:491

commit v5 on v4

--- a/solution.py
+++ b/solution.py
@@ -122,7 +122,7 @@
     far_up, far_dn, far_from_dn, far_from_up,
     norms, mate_in, chip_sum, chip_in,
     in_sem, data_sem, line_send, line_recv, near_send, near_recv, far_send, far_recv,
-    mate_send, mate_recv, chip_send, chip_recv, back_send, back_recv, ready,
+    mate_send, mate_recv, chip_send, chip_recv, cross_send, back_send, back_recv, ready,
 ):
     me_row, me_band = lax.axis_index("row"), lax.axis_index("band")
     core, chip = lax.rem(me_band, 2), me_band // 2
@@ -146,6 +146,12 @@
     for peer in peers:
         pl.when(peer > me_band)(functools.partial(greet, band=peer))
 
+    @pl.when(chip == 0)
+    def _():
+        for other in range(1, chip_count):
+            greet(band=2 * other + 1 - core)
+
+
     def fetch(source, target, sem):
         copy = pltpu.make_async_copy(source, target, sem)
         copy.start()
@@ -223,7 +229,7 @@
     q0, q1, cross = [lines_of(sym, part, 0) for part in range(3)]
     line_up[0] = lines_of(vec, 0, 0) + 0.5 * (q0 - (column_before(cross) - cross) + lines_of(grad, 0, 0))
     line_up[1] = lines_of(vec, 1, 0) + 0.5 * (cross - (column_before(q1) - q1) + lines_of(grad, 1, 0))
-    pl.semaphore_wait(barrier, 1 + chip + has_up.astype(jnp.int32) + has_down.astype(jnp.int32))
+    pl.semaphore_wait(barrier, 1 + chip + (chip > 0).astype(jnp.int32) + has_up.astype(jnp.int32) + has_down.astype(jnp.int32))
 
     def answer(peer):
         pl.semaphore_signal(ready, inc=1, device_id={"band": peer}, device_id_type=MESH)
@@ -304,8 +310,14 @@
 
     def chip_copy(which, peer, slot):
         return remote(
-            chip_sum.at[which], chip_in.at[which, slot],
-            chip_send.at[which, peer // 2], chip_recv.at[which, slot], band=peer,
+            chip_sum.at[which], chip_in.at[which, core, slot],
+            chip_send.at[which, peer // 2], chip_recv.at[which, core, slot], band=peer,
+        )
+
+    def cross_copy(which, half, slot):
+        return remote(
+            chip_sum.at[which], chip_in.at[which, half, slot],
+            cross_send.at[which], chip_recv.at[which, half, slot], band=1 - core,
         )
 
     def back_copy(which, half):
@@ -320,18 +332,32 @@
         mate_copy(which).wait()
         total = norms[which, core] + mate_in[which]
         chip_sum[which] = total
-        chip_in[which, chip] = total
+        chip_in[which, core, chip] = total
+        cross_copy(which, core, chip).start()
         for peer in peers:
             chip_copy(which, peer, chip).start()
+
+    def scale_half(which, half, bound):
+        total = chip_in[which, half, 0]
+        for other in range(1, chip_count):
+            total = total + chip_in[which, half, other]
+        scales[which, half] = 1.0 / jnp.maximum(1.0, jnp.sqrt(total) * (1.0 / bound))
 
     def send_scale(which, bound):
         for peer in peers:
             chip_copy(which, peer, peer // 2).wait()
-        total = chip_in[which, 0]
-        for other in range(1, chip_count):
-            total = total + chip_in[which, other]
-        scales[which, core] = 1.0 / jnp.maximum(1.0, jnp.sqrt(total) * (1.0 / bound))
-        back_copy(which, core).start()
+        scale_half(which, core, bound)
+        pl.when(chip > 0)(back_copy(which, core).start)
+
+    def other_scale(which, bound):
+        @pl.when(chip == 0)
+        def _():
+            for other in range(chip_count):
+                cross_copy(which, 1 - core, other).wait_recv()
+            scale_half(which, 1 - core, bound)
+
+        pl.when(chip > 0)(back_copy(which, 1 - core).wait)
+        cross_copy(which, core, chip).wait_send()
 
     norm_sym = lax.fori_loop(0, bands // 2, symmetric, jnp.zeros((rows, cols), F32))
     send_norm(0, norm_sym)
@@ -400,8 +426,8 @@
         return carry
 
     lax.fori_loop(0, chunks, finish, 0)
-    for which in range(2):
-        back_copy(which, 1 - core).wait()
+    other_scale(0, BOUND_SECOND)
+    other_scale(1, BOUND_FIRST)
 
 
 def finish_kernel(
@@ -477,12 +503,12 @@
         + [vmem(line, F32)] * 4
         + [vmem(near, F32)] * 4
         + [vmem(far, F32)] * 4
-        + [vmem((2, 2, *half), F32), vmem((2, *half), F32), vmem((2, *half), F32), vmem((2, band_axis // 2, *half), F32)]
+        + [vmem((2, 2, *half), F32), vmem((2, *half), F32), vmem((2, *half), F32), vmem((2, 2, band_axis // 2, *half), F32)]
         + [dma((11,)), dma((1,)), dma((2,)), dma((2,))]
         + [dma((2, chunks))] * 4
         + [dma((2,))] * 2
-        + [dma((2, band_axis // 2))] * 2
-        + [dma((2,))] * 2
+        + [dma((2, band_axis // 2)), dma((2, 2, band_axis // 2))]
+        + [dma((2,))] * 3
         + [pltpu.SemaphoreType.REGULAR],
         compiler_params=pltpu.CompilerParams(
             collective_id=0, has_side_effects=True, vmem_limit_bytes=24 * 1024 * 1024

time: 29.3 us -> 29.3 us (level)
  the two profiles are of different devices: /device:TPU:25 before, /device:TPU:153 now
where the time goes in v5:
time: 29.3 us; the launch traced here: 29.2 us
  Pallas kernels  28.5 us (97%)
  between operations  0.64 us (2%)
    pallas_call x1, Pallas kernels, body(): pl.pallas_call(functools.partial(kernel, bands, rows, cols, band_axis, ro...  26.3 us
    pallas_call x1, Pallas kernels, body(): pl.pallas_call(finish_kernel, out_shape=[hbm(a.shape, F32) for a in resul...  2.27 us

profile of v5, /device:TPU:153, one launch (start us, length us, event | category | flops | bytes accessed | tf_op | source)
XLA Modules:
  0.0 29.2 jit_solution(16740433482928118245)
XLA Ops:
  0.6 26.3 %shard_map.119 = (f32[16,16,512]{2,1,0:T(8,128)S(1)}, f32[2,16,16,512]{3,2,1,0:T(8,128)S(1)}, f32[2,16,16,512]{3,2,1,0:T(8,128)S(1)}, f32[3,16,16,512]{3,2,1,0:T...) custom-call(s32[16]{0:T(128)} %index_hbm.1, f32[15,16,15]{2,1,0:T(8,128)} %bitcast.1, ...), custom_call_target="tpu_custom_call" | custom-call | tf_op jit(solution)/shard_map/pallas_call | solution.py:490
  26.9 2.3 %shard_map.120 = (f32[16,16,512]{2,1,0:T(8,128)}, f32[2,16,16,512]{3,2,1,0:T(8,128)}, f32[2,16,16,512]{3,2,1,0:T(8,128)}, f32[3,16,16,512]{3,2,1,0:T(8,128)}, f32[16,16,512]{2,1,0:T(8,128)}) custom-call(f32[16,16,512]{2,1,0:T(8,128)S(1)} %get-tuple-element.11.img, f32[2,16,16,512]{3,2,1,0:T(8,128)S(1)} %get-tuple-element.12.vec, ...), custom_call_target="tpu_custom_call" | custom-call | tf_op jit(solution)/shard_map/pallas_call | solution.py:517
